TPU v7x, 32 devices: a whole 2x2x4 slice. The times are simulated.
32 devices in a mesh: roll: 4 (over x, core), tp: 8 (over z, y).
Axes of the slice: x: 2, y: 2, z: 4, core: 2. Of those that a mesh axis runs over, the one named last changes fastest.
Arguments:
- tokens: bfloat16 [128, 8, 2048], P(('roll', 'tp')), may hold values from -6 to 6
- lengths: int32 [128], P(('roll', 'tp')), may hold values from 1 to 8
- plan: int32 [2, 128, 1], P(None, ('roll', 'tp')), may hold values from 0 to 3, as said below
- owners: int32 [4], replicated, may hold values from 0 to 3, each once
- gate_up: float32 [4, 8, 2048, 768], P('roll', 'tp'), may hold values from -0.125 to 0.125
- down: float32 [4, 8, 384, 2048], P('roll', 'tp'), may hold values from -0.3125 to 0.3125
- norm_gain: float32 [2, 2048], replicated, may hold values from 0.5 to 1.5
- routing: int32 [2, 2048, 1], P(None, ('roll', 'tp')), may hold values from 0 to 7; in each aligned block of 64 rows (0 to 63, 64 to 127, ..., all dimensions but the last counted through in order) at most 10 rows name the same one
- route_weight: float32 [2, 2048], P(None, ('roll', 'tp')), may hold values from 0.1 to 1
Outputs:
- result: bfloat16 [128, 8, 2048], P(('roll', 'tp'))
Inputs may be any that keep to these rules, and one draw needn't show every extreme that they name: In layer 0 at most 2 rows of one device name the same owner, and every device's rows reach 2. For l >= 1, plan[l, i, 0] = (r + s_l[plan[l - 1, i, 0]]) mod 4, with r the roll index of row i's device and s_l a permutation of the owners drawn for layer l. owners is a permutation; layer l's master lies in the slot of roll index owners[l]. `routing`: every received token slot, empty ones included, names one window expert; of the 64 slots of one device at most 10 name the same expert, and in every draw some device reaches 10.
All inputs are finite; a program needn't handle non-finite values.
Results may differ from a plain program's by a relative error of at most 0.0048.
Values may be sent and summed in bfloat16 or wider, within the bound.
A program may use at most 128 MiB of HBM per device.

v0:
```python
import jax
import jax.numpy as jnp
from jax import lax
from jax.sharding import PartitionSpec as P

CAP = 2
epsilon = 1e-06


def spread(block, axis, owner):
    block = jnp.where(lax.axis_index(axis) == owner, block, jnp.zeros_like(block))
    return lax.psum(block, axis)


def slot_plan(target, groups, capacity):
    onehot = (target[:, None] == jnp.arange(groups, dtype=jnp.int32)[None, :]).astype(jnp.int32)
    before = jnp.cumsum(onehot, axis=0) - onehot
    within = jnp.sum(before * onehot, axis=1)
    target_slot = target * capacity + within
    item_count = target.shape[0]
    source = (
        jnp.zeros((groups * capacity,), jnp.int32)
        .at[target_slot]
        .set(jnp.arange(item_count, dtype=jnp.int32))
    )
    filled = jnp.zeros((groups * capacity,), jnp.bool_).at[target_slot].set(True)
    return (target_slot, source, filled)


def fetch_layer(gate_up, down, owners, layer_index):
    local_slot = (gate_up[0, 0].astype(jnp.bfloat16), down[0, 0].astype(jnp.bfloat16))
    return (
        spread(local_slot[0], "roll", owners[layer_index]),
        spread(local_slot[1], "roll", owners[layer_index]),
    )


def send_rows_out(current, meta_rows, source, filled, roll_size):
    row_tokens = current.shape[1]
    model_width = current.shape[2]
    send_rows = jnp.where(filled[:, None, None], current[source], jnp.zeros((), current.dtype))
    send_rows = send_rows.reshape(roll_size, CAP, row_tokens, model_width)
    send_meta = jnp.where(filled[:, None], meta_rows[source], -1)
    send_meta = send_meta.reshape(roll_size, CAP, meta_rows.shape[1])
    got_rows, got_meta = (
        lax.all_to_all(send_rows, "roll", split_axis=0, concat_axis=0, tiled=True),
        lax.all_to_all(send_meta, "roll", split_axis=0, concat_axis=0, tiled=True),
    )
    return (got_rows.reshape(-1, row_tokens, model_width), got_meta.reshape(-1, meta_rows.shape[1]))


def send_home(combined, target_slot, roll_size):
    row_tokens = combined.shape[1]
    model_width = combined.shape[2]
    home_rows = lax.all_to_all(
        combined.reshape(roll_size, CAP, row_tokens, model_width),
        "roll",
        split_axis=0,
        concat_axis=0,
        tiled=True,
    )
    return home_rows.reshape(roll_size * CAP, row_tokens, model_width)[target_slot]


def process_rows(held, held_lengths, weights, layer_gain, route_column, weight_column):
    tp_size = lax.axis_size("tp")
    row_tokens = held.shape[1]
    model_width = held.shape[2]
    received = held.reshape(-1, model_width)
    token_count = received.shape[0]
    present = (jnp.arange(row_tokens)[None, :] < held_lengths[:, None]).reshape(-1)
    widened = received.astype(jnp.float32)
    normed = (
        widened
        * lax.rsqrt(jnp.mean(widened * widened, axis=1, keepdims=True) + epsilon)
        * layer_gain[None, :]
    ).astype(jnp.bfloat16)
    expert_slots = 5 * token_count // (4 * tp_size)
    expert_target, expert_source, expert_filled = slot_plan(route_column, tp_size, expert_slots)
    send_tokens = jnp.where(
        expert_filled[:, None], normed[expert_source], jnp.zeros((), normed.dtype)
    )
    send_tokens = send_tokens.reshape(tp_size, expert_slots, model_width)
    gate_up_w, down_w = weights
    hidden_width = down_w.shape[0]
    arrived = lax.all_to_all(send_tokens, "tp", split_axis=0, concat_axis=0, tiled=True)
    flattened = arrived.reshape(-1, model_width)
    projected = jnp.dot(flattened, gate_up_w, preferred_element_type=jnp.float32)
    hidden = (jax.nn.silu(projected[:, :hidden_width]) * projected[:, hidden_width:]).astype(
        jnp.bfloat16
    )
    produced = jnp.dot(hidden, down_w, preferred_element_type=jnp.float32).astype(jnp.bfloat16)
    returned = lax.all_to_all(
        produced.reshape(arrived.shape), "tp", split_axis=0, concat_axis=0, tiled=True
    )
    answer = returned.reshape(-1, model_width)[expert_target]
    combined = (
        widened
        + (present.astype(jnp.float32) * weight_column)[:, None] * answer.astype(jnp.float32)
    ).astype(jnp.bfloat16)
    return combined.reshape(held.shape)


def per_device(tokens, lengths, plan, owners, gate_up, down, norm_gain, routing, route_weight):
    layer_count = plan.shape[0]
    roll_size = lax.axis_size("roll")
    plans = [
        slot_plan(plan[layer_index, :, 0], roll_size, CAP) for layer_index in range(layer_count)
    ]
    current = tokens
    for layer_index in range(layer_count):
        held, held_meta = send_rows_out(
            current, lengths[:, None], plans[layer_index][1], plans[layer_index][2], roll_size
        )
        combined = process_rows(
            held,
            held_meta[:, 0],
            fetch_layer(gate_up, down, owners, layer_index),
            norm_gain[layer_index],
            routing[layer_index, :, 0],
            route_weight[layer_index],
        )
        current = send_home(combined, plans[layer_index][0], roll_size)
    return current


def solution(mesh):
    in_specs = (
        P(("roll", "tp"), None, None),
        P(("roll", "tp")),
        P(None, ("roll", "tp"), None),
        P(),
        P("roll", "tp", None, None),
        P("roll", "tp", None, None),
        P(),
        P(None, ("roll", "tp"), None),
        P(None, ("roll", "tp")),
    )
    out_specs = P(("roll", "tp"), None, None)
    return jax.shard_map(
        per_device, mesh=mesh, in_specs=in_specs, out_specs=out_specs, check_vma=False
    )
```

profile of v0, /device:TPU:0, one launch (start us, length us, event | category | flops | bytes accessed | tf_op | source)
XLA Modules:
  0.0 311.0 jit_solution(11454669175080193429)
XLA Ops:
  6.5 1.4 fusion.41
  9.3 3.9 %select_bitcast_fusion.3 = (bf16[384,2048]{1,0:T(8,128)(2,1)}, bf16[384,2048]{1,0:T(8,128)(2,1)}) fusion(pred[]{:T(512)S(6)} %eq.80, f32[1,1,384,2048]{3,2,1,0:T(8,128)} %param.14, pred[]{:T(512)S(6)} %eq.85), kind=kLoop, calls=%fused_computation.23 | loop fusion | flops 2359296 | bytes 6291458 | tf_op jit(solution)/shard_map/jit(_where)/select_n | solution.py:11
  13.2 0.9 copy-done.2
  14.1 3.1 select_bitcast_fusion
  21.0 4.2 %all-to-all-start = ((bf16[4,2,8,2048]{3,2,1,0:T(8,128)(2,1)}), bf16[4,2,8,2048]{3,2,1,0:T(8,128)(2,1)S(1)}, u32[]{:S(2)}, u32[]{:S(2)}) async-start(bf16[4,2,8,2048]{3,2,1,0:T(8,128)(2,1)} %broadcast_select_fusion.2), calls=%async_computation | async-start | bytes 524288 | tf_op jit(solution)/shard_map/all_to_all | solution.py:46
  27.5 6.7 %all-to-all-done = bf16[4,2,8,2048]{3,2,1,0:T(8,128)(2,1)S(1)} async-done(((bf16[4,2,8,2048]{3,2,1,0:T(8,128)(2,1)}), bf16[4,2,8,2048]{3,2,1,0:T(8,128)(2,1)S(1)}, u32[]{:S(2)}, u32[]{:S(2)}) %all-to-all-start) | async-done | bytes 262176 | tf_op jit(solution)/shard_map/all_to_all | solution.py:46
  36.4 6.6 %all-to-all-start.2 = ((bf16[8,10,2048]{2,1,0:T(8,128)(2,1)}), bf16[8,10,2048]{2,1,0:T(8,128)(2,1)S(1)}, u32[]{:S(2)}, u32[]{:S(2)}) async-start(bf16[8,10,2048]{2,1,0:T(8,128)(2,1)} %broadcast_select_fusion.1), calls=%async_computation.2 | async-start | bytes 1048576 | tf_op jit(solution)/shard_map/all_to_all | solution.py:86
  44.4 13.0 %all-to-all-done.2 = bf16[8,10,2048]{2,1,0:T(8,128)(2,1)S(1)} async-done(((bf16[8,10,2048]{2,1,0:T(8,128)(2,1)}), bf16[8,10,2048]{2,1,0:T(8,128)(2,1)S(1)}, u32[]{:S(2)}, u32[]{:S(2)}) %all-to-all-start.2) | async-done | bytes 327712 | tf_op jit(solution)/shard_map/all_to_all | solution.py:86
  57.4 3.2 %all-to-all-start.1 = ((s32[4,2,1]{1,2,0:T(1,128)}), s32[4,2,1]{1,2,0:T(1,128)S(1)}, u32[]{:S(2)}, u32[]{:S(2)}) async-start(s32[4,2,1]{1,2,0:T(1,128)} %bitcast.9), calls=%async_computation.1 | async-start | bytes 4096 | tf_op jit(solution)/shard_map/all_to_all | solution.py:47
  60.7 133.1 %all-reduce.3.cloned.1.call-done = (bf16[384,2048]{1,0:T(8,128)(2,1)}, bf16[384,2048]{1,0:T(8,128)(2,1)}, bf16[2048,768]{1,0:T(8,128)(2,1)}, bf16[2048,768]{1,0:T(8,128)(2,1)}) async-done(((bf16[384,2048]{1,0:T(8,128)(2,1)}, bf16[384,2048]{1,0:T(8,128)(2,1)}, bf16[2048,768]{1,0:T(8,128)(2,1)}, bf16[2048,768]{1,0:T(8,128)(2,1)}), (bf16[384,2048]{1,0:T(8,128)(2,1)}, bf16[384,2048]{1,0:T(8,128)(2,1)}, ...) | async-done | bytes 9437200 | tf_op jit(solution)/shard_map/psum | solution.py:12
  193.8 2.7 fusion.42
  196.9 0.9 reshape.292
  197.8 5.5 %all-to-all-start.3 = ((bf16[8,10,2048]{2,1,0:T(8,128)(2,1)}), bf16[8,10,2048]{2,1,0:T(8,128)(2,1)S(1)}, u32[]{:S(2)}, u32[]{:S(2)}) async-start(bf16[8,10,2048]{2,1,0:T(8,128)(2,1)} %reshape.292), calls=%async_computation.3 | async-start | bytes 1048576 | tf_op jit(solution)/shard_map/all_to_all | solution.py:93
  206.2 11.5 %all-to-all-done.3 = bf16[8,10,2048]{2,1,0:T(8,128)(2,1)S(1)} async-done(((bf16[8,10,2048]{2,1,0:T(8,128)(2,1)}), bf16[8,10,2048]{2,1,0:T(8,128)(2,1)S(1)}, u32[]{:S(2)}, u32[]{:S(2)}) %all-to-all-start.3) | async-done | bytes 327712 | tf_op jit(solution)/shard_map/all_to_all | solution.py:93
  219.4 3.4 %all-to-all-start.4 = ((bf16[4,2,8,2048]{3,2,1,0:T(8,128)(2,1)}), bf16[4,2,8,2048]{3,2,1,0:T(8,128)(2,1)S(1)}, u32[]{:S(2)}, u32[]{:S(2)}) async-start(bf16[4,2,8,2048]{3,2,1,0:T(8,128)(2,1)} %fusion.3), calls=%async_computation.4 | async-start | bytes 524288 | tf_op jit(solution)/shard_map/all_to_all | solution.py:55
  222.9 6.0 %all-to-all-done.4 = bf16[4,2,8,2048]{3,2,1,0:T(8,128)(2,1)S(1)} async-done(((bf16[4,2,8,2048]{3,2,1,0:T(8,128)(2,1)}), bf16[4,2,8,2048]{3,2,1,0:T(8,128)(2,1)S(1)}, u32[]{:S(2)}, u32[]{:S(2)}) %all-to-all-start.4) | async-done | bytes 262176 | tf_op jit(solution)/shard_map/all_to_all | solution.py:55
  230.8 3.4 %all-to-all-start.5 = ((bf16[4,2,8,2048]{3,2,1,0:T(8,128)(2,1)}), bf16[4,2,8,2048]{3,2,1,0:T(8,128)(2,1)S(1)}, u32[]{:S(2)}, u32[]{:S(2)}) async-start(bf16[4,2,8,2048]{3,2,1,0:T(8,128)(2,1)} %broadcast_select_fusion.3), calls=%async_computation.5 | async-start | bytes 524288 | tf_op jit(solution)/shard_map/all_to_all | solution.py:46
  235.6 4.5 %all-to-all-done.5 = bf16[4,2,8,2048]{3,2,1,0:T(8,128)(2,1)S(1)} async-done(((bf16[4,2,8,2048]{3,2,1,0:T(8,128)(2,1)}), bf16[4,2,8,2048]{3,2,1,0:T(8,128)(2,1)S(1)}, u32[]{:S(2)}, u32[]{:S(2)}) %all-to-all-start.5) | async-done | bytes 262176 | tf_op jit(solution)/shard_map/all_to_all | solution.py:46
  240.6 1.5 gather_fusion.7
  242.1 2.0 gather.55
  244.1 2.0 broadcast_select_fusion
  246.1 4.1 %all-to-all-start.7 = ((bf16[8,10,2048]{2,1,0:T(8,128)(2,1)}), bf16[8,10,2048]{2,1,0:T(8,128)(2,1)}, u32[]{:S(2)}, u32[]{:S(2)}) async-start(bf16[8,10,2048]{2,1,0:T(8,128)(2,1)} %broadcast_select_fusion), calls=%async_computation.7 | async-start | bytes 1048576 | tf_op jit(solution)/shard_map/all_to_all | solution.py:86
  250.2 1.2 gather_fusion.6
  252.7 12.1 %all-to-all-done.7 = bf16[8,10,2048]{2,1,0:T(8,128)(2,1)} async-done(((bf16[8,10,2048]{2,1,0:T(8,128)(2,1)}), bf16[8,10,2048]{2,1,0:T(8,128)(2,1)}, u32[]{:S(2)}, u32[]{:S(2)}) %all-to-all-start.7) | async-done | bytes 327712 | tf_op jit(solution)/shard_map/all_to_all | solution.py:86
  264.8 3.2 %all-to-all-start.6 = ((s32[4,2,1]{1,2,0:T(1,128)}), s32[4,2,1]{1,2,0:T(1,128)S(1)}, u32[]{:S(2)}, u32[]{:S(2)}) async-start(s32[4,2,1]{1,2,0:T(1,128)} %bitcast.23), calls=%async_computation.6 | async-start | bytes 4096 | tf_op jit(solution)/shard_map/all_to_all | solution.py:47
  268.0 1.9 reshape.296
  269.9 1.7 fusion.43
  273.0 3.6 %all-to-all-start.8 = ((bf16[8,10,2048]{2,1,0:T(8,128)(2,1)}), bf16[8,10,2048]{2,1,0:T(8,128)(2,1)S(1)}, u32[]{:S(2)}, u32[]{:S(2)}) async-start(bf16[8,10,2048]{2,1,0:T(8,128)(2,1)} %reshape.297), calls=%async_computation.8 | async-start | bytes 1048576 | tf_op jit(solution)/shard_map/all_to_all | solution.py:93
  276.8 15.0 %all-to-all-done.8 = bf16[8,10,2048]{2,1,0:T(8,128)(2,1)S(1)} async-done(((bf16[8,10,2048]{2,1,0:T(8,128)(2,1)}), bf16[8,10,2048]{2,1,0:T(8,128)(2,1)S(1)}, u32[]{:S(2)}, u32[]{:S(2)}) %all-to-all-start.8) | async-done | bytes 327712 | tf_op jit(solution)/shard_map/all_to_all | solution.py:93
  293.5 3.4 %all-to-all-start.9 = ((bf16[4,2,8,2048]{3,2,1,0:T(8,128)(2,1)}), bf16[4,2,8,2048]{3,2,1,0:T(8,128)(2,1)S(1)}, u32[]{:S(2)}, u32[]{:S(2)}) async-start(bf16[4,2,8,2048]{3,2,1,0:T(8,128)(2,1)} %fusion.1), calls=%async_computation.9 | async-start | bytes 524288 | tf_op jit(solution)/shard_map/all_to_all | solution.py:55
  296.9 6.0 %all-to-all-done.9 = bf16[4,2,8,2048]{3,2,1,0:T(8,128)(2,1)S(1)} async-done(((bf16[4,2,8,2048]{3,2,1,0:T(8,128)(2,1)}), bf16[4,2,8,2048]{3,2,1,0:T(8,128)(2,1)S(1)}, u32[]{:S(2)}, u32[]{:S(2)}) %all-to-all-start.9) | async-done | bytes 262176 | tf_op jit(solution)/shard_map/all_to_all | solution.py:55
  302.9 1.2 gather_fusion.9
  (108 shorter events, 22.8 us)
Async XLA Ops:
  6.5 13.1 %copy-start = (bf16[4,8,2048]{2,1,0:T(8,128)(2,1)S(1)}, bf16[4,8,2048]{2,1,0:T(8,128)(2,1)}, u32[]{:S(2)}) copy-start(bf16[4,8,2048]{2,1,0:T(8,128)(2,1)} %param.9) | copy-start | bytes 393220
  6.5 187.3 %all-reduce.3.cloned.1.call-start = ((), (), s32[]{:S(2)}) async-start(), calls=%async_computation.10 | async-start | bytes 18874368 | tf_op jit(solution)/shard_map/psum | solution.py:12
  9.3 4.9 %copy-start.2 = (f32[1,1,2048,768]{3,2,1,0:T(8,128)S(1)}, f32[1,1,2048,768]{3,2,1,0:T(8,128)}, u32[]{:S(2)}) copy-start(f32[1,1,2048,768]{3,2,1,0:T(8,128)} %param.13) | copy-start | bytes 18874372
  17.2 0.7 copy-start.7
  17.2 8.0 %copy-start.8 = (s32[2,64,1]{1,2,0:T(1,128)S(1)}, s32[2,64,1]{1,2,0:T(1,128)}, u32[]{:S(2)}) copy-start(s32[2,64,1]{1,2,0:T(1,128)} %param.16) | copy-start | bytes 1540
  17.2 9.4 %copy-start.6 = (f32[2,2048]{1,0:T(2,128)S(1)}, f32[2,2048]{1,0:T(2,128)}, u32[]{:S(2)}) copy-start(f32[2,2048]{1,0:T(2,128)} %param.15) | copy-start | bytes 49156
  21.0 13.2 %all-to-all-start = ((bf16[4,2,8,2048]{3,2,1,0:T(8,128)(2,1)}), bf16[4,2,8,2048]{3,2,1,0:T(8,128)(2,1)S(1)}, u32[]{:S(2)}, u32[]{:S(2)}) async-start(bf16[4,2,8,2048]{3,2,1,0:T(8,128)(2,1)} %broadcast_select_fusion.2), calls=%async_computation | async-start | bytes 524288 | tf_op jit(solution)/shard_map/all_to_all | solution.py:46
  34.5 8.5 %copy-start.1 = (s32[4]{0:T(128)S(1)}, s32[4]{0:T(128)}, u32[]{:S(2)}) copy-start(s32[4]{0:T(128)} %param.10) | copy-start | bytes 52
  36.4 20.9 %all-to-all-start.2 = ((bf16[8,10,2048]{2,1,0:T(8,128)(2,1)}), bf16[8,10,2048]{2,1,0:T(8,128)(2,1)S(1)}, u32[]{:S(2)}, u32[]{:S(2)}) async-start(bf16[8,10,2048]{2,1,0:T(8,128)(2,1)} %broadcast_select_fusion.1), calls=%async_computation.2 | async-start | bytes 1048576 | tf_op jit(solution)/shard_map/all_to_all | solution.py:86
  57.4 140.5 %all-to-all-start.1 = ((s32[4,2,1]{1,2,0:T(1,128)}), s32[4,2,1]{1,2,0:T(1,128)S(1)}, u32[]{:S(2)}, u32[]{:S(2)}) async-start(s32[4,2,1]{1,2,0:T(1,128)} %bitcast.9), calls=%async_computation.1 | async-start | bytes 4096 | tf_op jit(solution)/shard_map/all_to_all | solution.py:47
  193.8 2.7 copy-start.5
  193.8 9.5 %copy-start.10 = (f32[2,64]{1,0:T(2,128)S(1)}, f32[2,64]{1,0:T(2,128)}, u32[]{:S(2)}) copy-start(f32[2,64]{1,0:T(2,128)} %param.17) | copy-start | bytes 1540
  197.8 19.9 %all-to-all-start.3 = ((bf16[8,10,2048]{2,1,0:T(8,128)(2,1)}), bf16[8,10,2048]{2,1,0:T(8,128)(2,1)S(1)}, u32[]{:S(2)}, u32[]{:S(2)}) async-start(bf16[8,10,2048]{2,1,0:T(8,128)(2,1)} %reshape.292), calls=%async_computation.3 | async-start | bytes 1048576 | tf_op jit(solution)/shard_map/all_to_all | solution.py:93
  204.6 1.5 copy-start.11
  219.4 9.4 %all-to-all-start.4 = ((bf16[4,2,8,2048]{3,2,1,0:T(8,128)(2,1)}), bf16[4,2,8,2048]{3,2,1,0:T(8,128)(2,1)S(1)}, u32[]{:S(2)}, u32[]{:S(2)}) async-start(bf16[4,2,8,2048]{3,2,1,0:T(8,128)(2,1)} %fusion.3), calls=%async_computation.4 | async-start | bytes 524288 | tf_op jit(solution)/shard_map/all_to_all | solution.py:55
  230.8 9.4 %all-to-all-start.5 = ((bf16[4,2,8,2048]{3,2,1,0:T(8,128)(2,1)}), bf16[4,2,8,2048]{3,2,1,0:T(8,128)(2,1)S(1)}, u32[]{:S(2)}, u32[]{:S(2)}) async-start(bf16[4,2,8,2048]{3,2,1,0:T(8,128)(2,1)} %broadcast_select_fusion.3), calls=%async_computation.5 | async-start | bytes 524288 | tf_op jit(solution)/shard_map/all_to_all | solution.py:46
  242.1 27.8 %copy-start.3 = (bf16[2048,768]{1,0:T(8,128)(2,1)S(1)}, bf16[2048,768]{1,0:T(8,128)(2,1)}, u32[]{:S(2)}) copy-start(bf16[2048,768]{1,0:T(8,128)(2,1)} %get-tuple-element.10) | copy-start | bytes 9437188
  246.1 18.7 %all-to-all-start.7 = ((bf16[8,10,2048]{2,1,0:T(8,128)(2,1)}), bf16[8,10,2048]{2,1,0:T(8,128)(2,1)}, u32[]{:S(2)}, u32[]{:S(2)}) async-start(bf16[8,10,2048]{2,1,0:T(8,128)(2,1)} %broadcast_select_fusion), calls=%async_computation.7 | async-start | bytes 1048576 | tf_op jit(solution)/shard_map/all_to_all | solution.py:86
  264.8 8.2 %all-to-all-start.6 = ((s32[4,2,1]{1,2,0:T(1,128)}), s32[4,2,1]{1,2,0:T(1,128)S(1)}, u32[]{:S(2)}, u32[]{:S(2)}) async-start(s32[4,2,1]{1,2,0:T(1,128)} %bitcast.23), calls=%async_computation.6 | async-start | bytes 4096 | tf_op jit(solution)/shard_map/all_to_all | solution.py:47
  269.9 1.7 copy-start.4
  269.9 6.7 %copy-start.9 = (f32[64]{0:T(128)S(1)}, f32[64]{0:T(128)}, u32[]{:S(2)}) copy-start(f32[64]{0:T(128)} %get-tuple-element.5) | copy-start | bytes 772
  273.0 18.8 %all-to-all-start.8 = ((bf16[8,10,2048]{2,1,0:T(8,128)(2,1)}), bf16[8,10,2048]{2,1,0:T(8,128)(2,1)S(1)}, u32[]{:S(2)}, u32[]{:S(2)}) async-start(bf16[8,10,2048]{2,1,0:T(8,128)(2,1)} %reshape.297), calls=%async_computation.8 | async-start | bytes 1048576 | tf_op jit(solution)/shard_map/all_to_all | solution.py:93
  293.5 9.4 %all-to-all-start.9 = ((bf16[4,2,8,2048]{3,2,1,0:T(8,128)(2,1)}), bf16[4,2,8,2048]{3,2,1,0:T(8,128)(2,1)S(1)}, u32[]{:S(2)}, u32[]{:S(2)}) async-start(bf16[4,2,8,2048]{3,2,1,0:T(8,128)(2,1)} %fusion.1), calls=%async_computation.9 | async-start | bytes 524288 | tf_op jit(solution)/shard_map/all_to_all | solution.py:55
Sparse Core Ops, SparseCore 0:
  17.4 176.4 all-reduce.2
where the time goes:
time: 312 us; the launch traced here: 311 us
  waiting for transfers between devices  208 us (67%)
  starting transfers between devices  40.7 us (13%)
  local copies, waits for them, and re-layouts  26.3 us (8%)
  other arithmetic  15.6 us (5%)
  between operations  15.1 us (5%)
  matrix products  5.22 us (2%)
    psum x1, waiting for transfers between devices, spread(): return lax.psum(block, axis)  133 us
    all_to_all x2, waiting for transfers between devices, process_rows(): lax.all_to_all(produced.reshape(arrived.shape), 'tp', split_axis=0, conca...  26.5 us
    all_to_all x2, waiting for transfers between devices, process_rows(): lax.all_to_all(send_tokens, 'tp', split_axis=0, concat_axis=0, tiled=True)  25.1 us
    all_to_all x2, waiting for transfers between devices, send_home(): lax.all_to_all(combined.reshape(roll_size, CAP, row_tokens, model_width),...  12 us
    all_to_all x2, waiting for transfers between devices, send_rows_out(): lax.all_to_all(send_rows, 'roll', split_axis=0, concat_axis=0, tiled=True)  11.3 us
    all_to_all x2, starting transfers between devices, process_rows(): lax.all_to_all(send_tokens, 'tp', split_axis=0, concat_axis=0, tiled=True)  10.7 us
    all_to_all x2, starting transfers between devices, process_rows(): lax.all_to_all(produced.reshape(arrived.shape), 'tp', split_axis=0, conca...  9.14 us
    all_to_all x2, starting transfers between devices, send_rows_out(): lax.all_to_all(send_rows, 'roll', split_axis=0, concat_axis=0, tiled=True)  7.61 us
  transfers between devices with their start and end apart: 11, of which 9 were waited for; matrix products, arithmetic and copies ran while one was open for 8% of the time, Pallas kernels for 0%

commit v1 on v0

--- a/solution.py
+++ b/solution.py
@@ -9,7 +9,7 @@
 
 def spread(block, axis, owner):
     block = jnp.where(lax.axis_index(axis) == owner, block, jnp.zeros_like(block))
-    return lax.psum(block, axis)
+    return jnp.sum(lax.all_gather(block, axis), axis=0)
 
 
 def slot_plan(target, groups, capacity):

time: 312 us -> 341 us (1.093)
  other arithmetic: 15.6 us -> 45.6 us
  local copies, waits for them, and re-layouts: 26.3 us -> 21.5 us
    all_gather x0 -> x4, waiting for transfers between devices: none -> 142 us  [spread(): return jnp.sum(lax.all_gather(block, axis), axis=0)]
    psum x1 -> x0, waiting for transfers between devices: 133 us -> none  [spread(): return lax.psum(block, axis)]
    reduce_sum x0 -> x4, other arithmetic: none -> 29.1 us  [spread(): return jnp.sum(lax.all_gather(block, axis), axis=0)]
    all_to_all x2, waiting for transfers between devices: 25.1 us -> 13 us  [process_rows(): lax.all_to_all(send_tokens, 'tp', split_axis=0, concat_axis=0, tiled=True)]
  transfers between devices with their start and end apart: 11 -> 14, of which waited for: 9 -> 10; matrix products, arithmetic and copies ran while one was open for 8% -> 19% of each run, Pallas kernels for 0% -> 0%
where the time goes in v1:
time: 341 us; the launch traced here: 340 us
  waiting for transfers between devices  211 us (62%)
  other arithmetic  45.6 us (13%)
  starting transfers between devices  42.6 us (12%)
  local copies, waits for them, and re-layouts  21.5 us (6%)
  between operations  14.9 us (4%)
  matrix products  4.34 us (1%)
    all_gather x4, waiting for transfers between devices, spread(): return jnp.sum(lax.all_gather(block, axis), axis=0)  142 us
    reduce_sum x4, other arithmetic, spread(): return jnp.sum(lax.all_gather(block, axis), axis=0)  29.1 us
    all_to_all x2, waiting for transfers between devices, process_rows(): lax.all_to_all(produced.reshape(arrived.shape), 'tp', split_axis=0, conca...  27.5 us
    all_to_all x2, waiting for transfers between devices, send_home(): lax.all_to_all(combined.reshape(roll_size, CAP, row_tokens, model_width),...  15.1 us
    all_to_all x2, waiting for transfers between devices, process_rows(): lax.all_to_all(send_tokens, 'tp', split_axis=0, concat_axis=0, tiled=True)  13 us
    all_to_all x2, waiting for transfers between devices, send_rows_out(): lax.all_to_all(send_rows, 'roll', split_axis=0, concat_axis=0, tiled=True)  11.9 us
    all_to_all x2, starting transfers between devices, process_rows(): lax.all_to_all(produced.reshape(arrived.shape), 'tp', split_axis=0, conca...  11 us
    all_to_all x2, starting transfers between devices, process_rows(): lax.all_to_all(send_tokens, 'tp', split_axis=0, concat_axis=0, tiled=True)  10.5 us
  transfers between devices with their start and end apart: 14, of which 10 were waited for; matrix products, arithmetic and copies ran while one was open for 19% of the time, Pallas kernels for 0%

profile of v1, /device:TPU:0, one launch (start us, length us, event | category | flops | bytes accessed | tf_op | source)
XLA Modules:
  0.0 339.6 jit_solution(15287888801577794617)
XLA Ops:
  6.5 1.4 fusion.41
  9.3 3.8 %broadcast_select_fusion.3 = (bf16[1,1,384,2048]{3,2,1,0:T(8,128)(2,1)}, bf16[1,1,384,2048]{3,2,1,0:T(8,128)(2,1)}) fusion(pred[]{:T(512)S(6)} %eq.80, f32[1,1,384,2048]{3,2,1,0:T(8,128)} %param.14, pred[]{:T(512)S(6)} %eq.85), kind=kLoop, calls=%fused_computation.23 | loop fusion | flops 2359296 | bytes 6291458 | tf_op jit(solution)/shard_map/jit(_where)/select_n | solution.py:11
  13.1 5.9 %broadcast_select_fusion = (bf16[1,1,2048,768]{3,2,1,0:T(8,128)(2,1)}, bf16[1,1,2048,768]{3,2,1,0:T(8,128)(2,1)}) fusion(pred[]{:T(512)S(6)} %eq.85, f32[1,1,2048,768]{3,2,1,0:T(8,128)} %param.13, pred[]{:T(512)S(6)} %eq.80), kind=kLoop, calls=%fused_computation.18 | loop fusion | flops 4718592 | bytes 12582914 | tf_op jit(solution)/shard_map/jit(_where)/select_n | solution.py:11
  23.5 4.2 %all-to-all-start = ((bf16[4,2,8,2048]{3,2,1,0:T(8,128)(2,1)}), bf16[4,2,8,2048]{3,2,1,0:T(8,128)(2,1)S(1)}, u32[]{:S(2)}, u32[]{:S(2)}) async-start(bf16[4,2,8,2048]{3,2,1,0:T(8,128)(2,1)} %broadcast_select_fusion.6), calls=%async_computation | async-start | bytes 524288 | tf_op jit(solution)/shard_map/all_to_all | solution.py:46
  30.0 6.9 %all-to-all-done = bf16[4,2,8,2048]{3,2,1,0:T(8,128)(2,1)S(1)} async-done(((bf16[4,2,8,2048]{3,2,1,0:T(8,128)(2,1)}), bf16[4,2,8,2048]{3,2,1,0:T(8,128)(2,1)S(1)}, u32[]{:S(2)}, u32[]{:S(2)}) %all-to-all-start) | async-done | bytes 262176 | tf_op jit(solution)/shard_map/all_to_all | solution.py:46
  39.2 6.4 %all-to-all-start.2 = ((bf16[8,10,2048]{2,1,0:T(8,128)(2,1)}), bf16[8,10,2048]{2,1,0:T(8,128)(2,1)S(1)}, u32[]{:S(2)}, u32[]{:S(2)}) async-start(bf16[8,10,2048]{2,1,0:T(8,128)(2,1)} %broadcast_select_fusion.5), calls=%async_computation.2 | async-start | bytes 1048576 | tf_op jit(solution)/shard_map/all_to_all | solution.py:86
  46.9 13.0 %all-to-all-done.2 = bf16[8,10,2048]{2,1,0:T(8,128)(2,1)S(1)} async-done(((bf16[8,10,2048]{2,1,0:T(8,128)(2,1)}), bf16[8,10,2048]{2,1,0:T(8,128)(2,1)S(1)}, u32[]{:S(2)}, u32[]{:S(2)}) %all-to-all-start.2) | async-done | bytes 327712 | tf_op jit(solution)/shard_map/all_to_all | solution.py:86
  59.9 3.2 all-to-all-start.1
  64.0 1.3 all-gather.11.cloned.1.call-done
  65.3 5.7 %reduce_sum.118 = bf16[384,2048]{1,0:T(8,128)(2,1)} reduce(bf16[4,1,384,2048]{3,2,1,0:T(8,128)(2,1)} %all-gather.11.cloned.1.call-done, bf16[]{:T(256)} %constant.55.clone.1), dimensions={0,1}, to_apply=%region_13.14 | reduce | flops 2359296 | bytes 7864322 | tf_op jit(solution)/shard_map/reduce_sum | solution.py:12
  71.0 78.0 %all-gather.9.cloned.1.call-done = bf16[4,1,2048,768]{3,2,1,0:T(8,128)(2,1)} async-done(((bf16[1,1,2048,768]{3,2,1,0:T(8,128)(2,1)}), bf16[4,1,2048,768]{3,2,1,0:T(8,128)(2,1)}) %all-gather.9.cloned.1.call-update) | async-done | bytes 12582928 | tf_op jit(solution)/shard_map/all_gather | solution.py:12
  149.0 8.6 %reduce_sum.117 = bf16[2048,768]{1,0:T(8,128)(2,1)S(1)} reduce(bf16[4,1,2048,768]{3,2,1,0:T(8,128)(2,1)} %all-gather.9.cloned.1.call-done, bf16[]{:T(256)} %constant.55.clone.1), dimensions={0,1}, to_apply=%region_12.13 | reduce | flops 4718592 | bytes 15728642 | tf_op jit(solution)/shard_map/reduce_sum | solution.py:12
  157.6 1.8 fusion.42
  160.7 5.5 %all-to-all-start.3 = ((bf16[8,10,2048]{2,1,0:T(8,128)(2,1)}), bf16[8,10,2048]{2,1,0:T(8,128)(2,1)S(1)}, u32[]{:S(2)}, u32[]{:S(2)}) async-start(bf16[8,10,2048]{2,1,0:T(8,128)(2,1)} %reshape.332), calls=%async_computation.3 | async-start | bytes 1048576 | tf_op jit(solution)/shard_map/all_to_all | solution.py:93
  168.6 12.5 %all-to-all-done.3 = bf16[8,10,2048]{2,1,0:T(8,128)(2,1)S(1)} async-done(((bf16[8,10,2048]{2,1,0:T(8,128)(2,1)}), bf16[8,10,2048]{2,1,0:T(8,128)(2,1)S(1)}, u32[]{:S(2)}, u32[]{:S(2)}) %all-to-all-start.3) | async-done | bytes 327712 | tf_op jit(solution)/shard_map/all_to_all | solution.py:93
  182.8 3.4 %all-to-all-start.4 = ((bf16[4,2,8,2048]{3,2,1,0:T(8,128)(2,1)}), bf16[4,2,8,2048]{3,2,1,0:T(8,128)(2,1)S(1)}, u32[]{:S(2)}, u32[]{:S(2)}) async-start(bf16[4,2,8,2048]{3,2,1,0:T(8,128)(2,1)} %fusion.3), calls=%async_computation.4 | async-start | bytes 524288 | tf_op jit(solution)/shard_map/all_to_all | solution.py:55
  186.3 9.1 %all-to-all-done.4 = bf16[4,2,8,2048]{3,2,1,0:T(8,128)(2,1)S(1)} async-done(((bf16[4,2,8,2048]{3,2,1,0:T(8,128)(2,1)}), bf16[4,2,8,2048]{3,2,1,0:T(8,128)(2,1)S(1)}, u32[]{:S(2)}, u32[]{:S(2)}) %all-to-all-start.4) | async-done | bytes 262176 | tf_op jit(solution)/shard_map/all_to_all | solution.py:55
  197.3 3.4 %all-to-all-start.5 = ((bf16[4,2,8,2048]{3,2,1,0:T(8,128)(2,1)}), bf16[4,2,8,2048]{3,2,1,0:T(8,128)(2,1)S(1)}, u32[]{:S(2)}, u32[]{:S(2)}) async-start(bf16[4,2,8,2048]{3,2,1,0:T(8,128)(2,1)} %broadcast_select_fusion.7), calls=%async_computation.5 | async-start | bytes 524288 | tf_op jit(solution)/shard_map/all_to_all | solution.py:46
  200.7 1.0 scatter_custom_fusion.6
  201.8 4.9 %all-to-all-done.5 = bf16[4,2,8,2048]{3,2,1,0:T(8,128)(2,1)S(1)} async-done(((bf16[4,2,8,2048]{3,2,1,0:T(8,128)(2,1)}), bf16[4,2,8,2048]{3,2,1,0:T(8,128)(2,1)S(1)}, u32[]{:S(2)}, u32[]{:S(2)}) %all-to-all-start.5) | async-done | bytes 262176 | tf_op jit(solution)/shard_map/all_to_all | solution.py:46
  208.9 4.1 %all-to-all-start.7 = ((bf16[8,10,2048]{2,1,0:T(8,128)(2,1)}), bf16[8,10,2048]{2,1,0:T(8,128)(2,1)}, u32[]{:S(2)}, u32[]{:S(2)}) async-start(bf16[8,10,2048]{2,1,0:T(8,128)(2,1)} %broadcast_select_fusion.4), calls=%async_computation.7 | async-start | bytes 1048576 | tf_op jit(solution)/shard_map/all_to_all | solution.py:86
  214.4 6.2 %reduce_sum.123 = bf16[384,2048]{1,0:T(8,128)(2,1)} reduce(bf16[4,1,384,2048]{3,2,1,0:T(8,128)(2,1)} %all-gather.15.cloned.1.call-done, bf16[]{:T(256)} %constant.55.clone.1), dimensions={0,1}, to_apply=%region_21.22 | reduce | flops 2359296 | bytes 7864322 | tf_op jit(solution)/shard_map/reduce_sum | solution.py:12
  220.6 62.7 %all-gather.13.cloned.1.call-done = bf16[4,1,2048,768]{3,2,1,0:T(8,128)(2,1)} async-done(((bf16[1,1,2048,768]{3,2,1,0:T(8,128)(2,1)}), bf16[4,1,2048,768]{3,2,1,0:T(8,128)(2,1)}) %all-gather.13.cloned.1.call-update) | async-done | bytes 12582928 | tf_op jit(solution)/shard_map/all_gather | solution.py:12
  283.3 8.6 %reduce_sum.122 = bf16[2048,768]{1,0:T(8,128)(2,1)S(1)} reduce(bf16[4,1,2048,768]{3,2,1,0:T(8,128)(2,1)} %all-gather.13.cloned.1.call-done, bf16[]{:T(256)} %constant.55.clone.1), dimensions={0,1}, to_apply=%region_20.21 | reduce | flops 4718592 | bytes 15728642 | tf_op jit(solution)/shard_map/reduce_sum | solution.py:12
  291.9 3.2 all-to-all-start.6
  295.2 1.9 reshape.336
  297.0 1.7 fusion.43
  300.1 5.5 %all-to-all-start.8 = ((bf16[8,10,2048]{2,1,0:T(8,128)(2,1)}), bf16[8,10,2048]{2,1,0:T(8,128)(2,1)S(1)}, u32[]{:S(2)}, u32[]{:S(2)}) async-start(bf16[8,10,2048]{2,1,0:T(8,128)(2,1)} %reshape.337), calls=%async_computation.8 | async-start | bytes 1048576 | tf_op jit(solution)/shard_map/all_to_all | solution.py:93
  305.8 15.0 %all-to-all-done.8 = bf16[8,10,2048]{2,1,0:T(8,128)(2,1)S(1)} async-done(((bf16[8,10,2048]{2,1,0:T(8,128)(2,1)}), bf16[8,10,2048]{2,1,0:T(8,128)(2,1)S(1)}, u32[]{:S(2)}, u32[]{:S(2)}) %all-to-all-start.8) | async-done | bytes 327712 | tf_op jit(solution)/shard_map/all_to_all | solution.py:93
  322.5 3.4 %all-to-all-start.9 = ((bf16[4,2,8,2048]{3,2,1,0:T(8,128)(2,1)}), bf16[4,2,8,2048]{3,2,1,0:T(8,128)(2,1)S(1)}, u32[]{:S(2)}, u32[]{:S(2)}) async-start(bf16[4,2,8,2048]{3,2,1,0:T(8,128)(2,1)} %fusion.1), calls=%async_computation.9 | async-start | bytes 524288 | tf_op jit(solution)/shard_map/all_to_all | solution.py:55
  325.9 6.0 %all-to-all-done.9 = bf16[4,2,8,2048]{3,2,1,0:T(8,128)(2,1)S(1)} async-done(((bf16[4,2,8,2048]{3,2,1,0:T(8,128)(2,1)}), bf16[4,2,8,2048]{3,2,1,0:T(8,128)(2,1)S(1)}, u32[]{:S(2)}, u32[]{:S(2)}) %all-to-all-start.9) | async-done | bytes 262176 | tf_op jit(solution)/shard_map/all_to_all | solution.py:55
  331.9 1.2 gather_fusion.9
  (117 shorter events, 25.1 us)
Async XLA Ops:
  6.5 15.6 %copy-start = (bf16[4,8,2048]{2,1,0:T(8,128)(2,1)S(1)}, bf16[4,8,2048]{2,1,0:T(8,128)(2,1)}, u32[]{:S(2)}) copy-start(bf16[4,8,2048]{2,1,0:T(8,128)(2,1)} %param.9) | copy-start | bytes 393220
  6.5 58.7 %all-gather.11.cloned.1.call-start = ((), (), s32[]{:S(2)}) async-start(), calls=%async_computation.11 | async-start | bytes 7864320 | tf_op jit(solution)/shard_map/all_gather | solution.py:12
  13.1 135.9 %all-gather.9.cloned.1.call-start = ((), (), s32[]{:S(2)}) async-start(), calls=%async_computation.10 | async-start | bytes 15728640 | tf_op jit(solution)/shard_map/all_gather | solution.py:12
  19.0 1.3 copy-start.6
  19.0 195.3 %all-gather.15.cloned.1.call-start = ((), (), s32[]{:S(2)}) async-start(), calls=%async_computation.13 | async-start | bytes 7864320 | tf_op jit(solution)/shard_map/all_gather | solution.py:12
  19.1 8.6 %copy-start.7 = (s32[2,64,1]{1,2,0:T(1,128)S(1)}, s32[2,64,1]{1,2,0:T(1,128)}, u32[]{:S(2)}) copy-start(s32[2,64,1]{1,2,0:T(1,128)} %param.16) | copy-start | bytes 1540
  19.1 10.0 %copy-start.5 = (f32[2,2048]{1,0:T(2,128)S(1)}, f32[2,2048]{1,0:T(2,128)}, u32[]{:S(2)}) copy-start(f32[2,2048]{1,0:T(2,128)} %param.15) | copy-start | bytes 49156
  19.8 263.5 %all-gather.13.cloned.1.call-start = ((), (), s32[]{:S(2)}) async-start(), calls=%async_computation.12 | async-start | bytes 15728640 | tf_op jit(solution)/shard_map/all_gather | solution.py:12
  20.8 1.3 copy-start.9
  23.5 13.4 %all-to-all-start = ((bf16[4,2,8,2048]{3,2,1,0:T(8,128)(2,1)}), bf16[4,2,8,2048]{3,2,1,0:T(8,128)(2,1)S(1)}, u32[]{:S(2)}, u32[]{:S(2)}) async-start(bf16[4,2,8,2048]{3,2,1,0:T(8,128)(2,1)} %broadcast_select_fusion.6), calls=%async_computation | async-start | bytes 524288 | tf_op jit(solution)/shard_map/all_to_all | solution.py:46
  37.2 8.4 %copy-start.2 = (s32[4]{0:T(128)S(1)}, s32[4]{0:T(128)}, u32[]{:S(2)}) copy-start(s32[4]{0:T(128)} %param.10) | copy-start | bytes 52
  39.2 20.7 %all-to-all-start.2 = ((bf16[8,10,2048]{2,1,0:T(8,128)(2,1)}), bf16[8,10,2048]{2,1,0:T(8,128)(2,1)S(1)}, u32[]{:S(2)}, u32[]{:S(2)}) async-start(bf16[8,10,2048]{2,1,0:T(8,128)(2,1)} %broadcast_select_fusion.5), calls=%async_computation.2 | async-start | bytes 1048576 | tf_op jit(solution)/shard_map/all_to_all | solution.py:86
  59.9 100.8 %all-to-all-start.1 = ((s32[4,2,1]{1,2,0:T(1,128)}), s32[4,2,1]{1,2,0:T(1,128)S(1)}, u32[]{:S(2)}, u32[]{:S(2)}) async-start(s32[4,2,1]{1,2,0:T(1,128)} %bitcast.9), calls=%async_computation.1 | async-start | bytes 4096 | tf_op jit(solution)/shard_map/all_to_all | solution.py:47
  157.6 1.8 copy-start.4
  157.6 8.6 %copy-start.8 = (f32[2,64]{1,0:T(2,128)S(1)}, f32[2,64]{1,0:T(2,128)}, u32[]{:S(2)}) copy-start(f32[2,64]{1,0:T(2,128)} %param.17) | copy-start | bytes 1540
  160.7 20.4 %all-to-all-start.3 = ((bf16[8,10,2048]{2,1,0:T(8,128)(2,1)}), bf16[8,10,2048]{2,1,0:T(8,128)(2,1)S(1)}, u32[]{:S(2)}, u32[]{:S(2)}) async-start(bf16[8,10,2048]{2,1,0:T(8,128)(2,1)} %reshape.332), calls=%async_computation.3 | async-start | bytes 1048576 | tf_op jit(solution)/shard_map/all_to_all | solution.py:93
  182.8 12.5 %all-to-all-start.4 = ((bf16[4,2,8,2048]{3,2,1,0:T(8,128)(2,1)}), bf16[4,2,8,2048]{3,2,1,0:T(8,128)(2,1)S(1)}, u32[]{:S(2)}, u32[]{:S(2)}) async-start(bf16[4,2,8,2048]{3,2,1,0:T(8,128)(2,1)} %fusion.3), calls=%async_computation.4 | async-start | bytes 524288 | tf_op jit(solution)/shard_map/all_to_all | solution.py:55
  197.3 9.4 %all-to-all-start.5 = ((bf16[4,2,8,2048]{3,2,1,0:T(8,128)(2,1)}), bf16[4,2,8,2048]{3,2,1,0:T(8,128)(2,1)S(1)}, u32[]{:S(2)}, u32[]{:S(2)}) async-start(bf16[4,2,8,2048]{3,2,1,0:T(8,128)(2,1)} %broadcast_select_fusion.7), calls=%async_computation.5 | async-start | bytes 524288 | tf_op jit(solution)/shard_map/all_to_all | solution.py:46
  208.9 83.0 %all-to-all-start.7 = ((bf16[8,10,2048]{2,1,0:T(8,128)(2,1)}), bf16[8,10,2048]{2,1,0:T(8,128)(2,1)}, u32[]{:S(2)}, u32[]{:S(2)}) async-start(bf16[8,10,2048]{2,1,0:T(8,128)(2,1)} %broadcast_select_fusion.4), calls=%async_computation.7 | async-start | bytes 1048576 | tf_op jit(solution)/shard_map/all_to_all | solution.py:86
  291.9 8.2 %all-to-all-start.6 = ((s32[4,2,1]{1,2,0:T(1,128)}), s32[4,2,1]{1,2,0:T(1,128)S(1)}, u32[]{:S(2)}, u32[]{:S(2)}) async-start(s32[4,2,1]{1,2,0:T(1,128)} %bitcast.21), calls=%async_computation.6 | async-start | bytes 4096 | tf_op jit(solution)/shard_map/all_to_all | solution.py:47
  297.0 1.7 copy-start.3
  299.2 33.9 %copy-start.1 = (bf16[4,8,2048]{2,1,0:T(8,128)(2,1)S(1)}, bf16[4,8,2048]{2,1,0:T(8,128)(2,1)}, u32[]{:S(2)}) copy-start(bf16[4,8,2048]{2,1,0:T(8,128)(2,1)} %param.9) | copy-start | bytes 393220
  300.1 20.6 %all-to-all-start.8 = ((bf16[8,10,2048]{2,1,0:T(8,128)(2,1)}), bf16[8,10,2048]{2,1,0:T(8,128)(2,1)S(1)}, u32[]{:S(2)}, u32[]{:S(2)}) async-start(bf16[8,10,2048]{2,1,0:T(8,128)(2,1)} %reshape.337), calls=%async_computation.8 | async-start | bytes 1048576 | tf_op jit(solution)/shard_map/all_to_all | solution.py:93
  322.5 9.4 %all-to-all-start.9 = ((bf16[4,2,8,2048]{3,2,1,0:T(8,128)(2,1)}), bf16[4,2,8,2048]{3,2,1,0:T(8,128)(2,1)S(1)}, u32[]{:S(2)}, u32[]{:S(2)}) async-start(bf16[4,2,8,2048]{3,2,1,0:T(8,128)(2,1)} %fusion.1), calls=%async_computation.9 | async-start | bytes 524288 | tf_op jit(solution)/shard_map/all_to_all | solution.py:55
Sparse Core Ops, SparseCore 0:
  13.2 52.0 all-gather.10
  66.8 82.0 all-gather.8
  150.5 49.1 all-gather.14
  201.2 82.0 all-gather.12
